TPU v7x, 768 devices: a whole 4x8x12 slice. The times are simulated.
768 devices in a mesh: dp: 16 (over y, core), expert: 48 (over z, x).
Axes of the slice: x: 4, y: 8, z: 12, core: 2. Of those that a mesh axis runs over, the one named last changes fastest.
Arguments:
- tokens: bfloat16 [6144, 8192], P('expert', 'dp'), may hold values from -6 to 6
- cotangent: bfloat16 [6144, 8192], P('expert', 'dp'), may hold values from -6 to 6
- routes: int32 [6144, 2], P('expert'), may hold values from 0 to 47, all different within a row; in each aligned block of 128 rows (0 to 127, 128 to 255, ...) at most 10 rows name the same one
- route_weight: float32 [6144, 2], P('expert'), may hold values from 0.25 to 1
- gate_dense: bfloat16 [18432, 8192], P('expert', 'dp'), may hold values from -0.0625 to 0.0625
- up_dense: bfloat16 [18432, 8192], P('expert', 'dp'), may hold values from -0.0625 to 0.0625
- down_dense: bfloat16 [18432, 8192], P('expert', 'dp'), may hold values from -0.3125 to 0.3125
- slice_map: int32 [18432], replicated, may hold values from 0 to 18431, as said below
Outputs:
- mixed: bfloat16 [6144, 8192], P('expert', 'dp')
- grad_gate: bfloat16 [18432, 8192], P('expert', 'dp')
- grad_up: bfloat16 [18432, 8192], P('expert', 'dp')
- grad_down: bfloat16 [18432, 8192], P('expert', 'dp')
Inputs may be any that keep to these rules, and one draw needn't show every extreme that they name: `slice_map`: A permutation of the dense rows: value v puts a row at position v % 384 of expert v // 384; the 384 rows of each index of expert give exactly 8 rows to every expert. `routes`: each row names 2 different experts; the 128 rows of one device name each expert at most 10 times.
All inputs are finite; a program needn't handle non-finite values.
Results may differ from a plain program's by a relative error of at most 0.0058.
Values may be sent and summed in bfloat16 or wider, within the bound.
A program may use at most 32 MiB of HBM per device.

v0:
```python
import jax
import jax.numpy as jnp
from jax import lax
from jax.sharding import PartitionSpec as P


def for_sending(value):

    def short(part):
        return part.astype(jnp.bfloat16) if part.dtype == jnp.float32 else part

    return jax.tree.map(short, value)


def local(tokens, cotangent, routes, route_weight, gate_dense, up_dense, down_dense, slice_map):
    owners = lax.axis_size("expert")
    here = lax.axis_index("expert")
    hidden_rows, width = gate_dense.shape
    tok_rows, topk = routes.shape
    group = hidden_rows // owners
    capacity = max(2, 2 * tok_rows * topk // owners)
    slots = owners * capacity
    block_map = lax.dynamic_slice_in_dim(slice_map, here * hidden_rows, hidden_rows)
    send_order = jnp.argsort(block_map // hidden_rows, stable=True)
    outgoing = tuple(
        (w[send_order].reshape(owners, group, width) for w in (gate_dense, up_dense, down_dense))
    )
    arrived = jax.tree.map(
        lambda part, own: part.astype(own.dtype),
        lax.all_to_all(for_sending(outgoing), "expert", split_axis=0, concat_axis=0, tiled=True),
        outgoing,
    )
    whole_map = slice_map.reshape(owners, hidden_rows)
    mine = whole_map // hidden_rows == here
    picked = jnp.argsort(jnp.where(mine, 0, 1).astype(jnp.int32), axis=1, stable=True)[:, :group]
    places = (jnp.take_along_axis(whole_map, picked, axis=1) % hidden_rows).reshape(-1)
    gate_w, up_w, down_w = (
        jnp.zeros((hidden_rows, width), jnp.bfloat16).at[places].set(a.reshape(-1, width))
        for a in arrived
    )
    flat = routes.reshape(-1)
    wflat = route_weight.reshape(-1)
    copies = tok_rows * topk
    onehot = (flat[:, None] == jnp.arange(owners, dtype=jnp.int32)[None, :]).astype(jnp.int32)
    ranks = jnp.sum((jnp.cumsum(onehot, axis=0) - onehot) * onehot, axis=1)
    target = flat * capacity + ranks
    slot_copy = (
        jnp.full((slots,), -1, jnp.int32).at[target].set(jnp.arange(copies, dtype=jnp.int32))
    )
    filled = slot_copy >= 0
    copy_index = jnp.maximum(slot_copy, 0)
    slot_token = copy_index // topk
    slot_weight = jnp.where(filled, wflat[copy_index], jnp.float32(0.0))
    send_x = jnp.where(filled[:, None], tokens[slot_token], jnp.zeros((), jnp.bfloat16))
    send_c = (slot_weight[:, None] * cotangent[slot_token].astype(jnp.float32)).astype(jnp.bfloat16)
    got_x, got_c = (
        lax.all_to_all(
            send_x.reshape(owners, capacity, width),
            "expert",
            split_axis=0,
            concat_axis=0,
            tiled=True,
        ),
        lax.all_to_all(
            send_c.reshape(owners, capacity, width),
            "expert",
            split_axis=0,
            concat_axis=0,
            tiled=True,
        ),
    )
    inputs = got_x.reshape(slots, width)
    cots = got_c.reshape(slots, width)
    contract = (((1,), (1,)), ((), ()))
    part_g = lax.dot_general(inputs, gate_w, contract, preferred_element_type=jnp.float32)
    part_u = lax.dot_general(inputs, up_w, contract, preferred_element_type=jnp.float32)
    part_q = lax.dot_general(cots, down_w, contract, preferred_element_type=jnp.float32)
    gate, upval, backward_pass = lax.psum((part_g, part_u, part_q), "dp")
    sig = jax.nn.sigmoid(gate)
    hidden_state = (gate * sig * upval).astype(jnp.bfloat16)
    dgate = (backward_pass * upval * sig * (1.0 + gate * (1.0 - sig))).astype(jnp.bfloat16)
    dup = (backward_pass * gate * sig).astype(jnp.bfloat16)
    hidden_state, dgate, dup = (hidden_state, dgate, dup)
    layer_output = jnp.dot(hidden_state, down_w, preferred_element_type=jnp.float32).astype(
        jnp.bfloat16
    )
    rowsum = (((0,), (0,)), ((), ()))
    grad_g = lax.dot_general(dgate, inputs, rowsum, preferred_element_type=jnp.float32).astype(
        jnp.bfloat16
    )
    grad_u = lax.dot_general(dup, inputs, rowsum, preferred_element_type=jnp.float32).astype(
        jnp.bfloat16
    )
    grad_v = lax.dot_general(hidden_state, cots, rowsum, preferred_element_type=jnp.float32).astype(
        jnp.bfloat16
    )
    sent = (layer_output.reshape(owners, capacity, width),) + tuple(
        (g[places].reshape(owners, group, width) for g in (grad_g, grad_u, grad_v))
    )
    back_y, back_g, back_u, back_v = jax.tree.map(
        lambda part, own: part.astype(own.dtype),
        lax.all_to_all(for_sending(sent), "expert", split_axis=0, concat_axis=0, tiled=True),
        sent,
    )
    received = back_y.reshape(slots, width)
    weighted = slot_weight[:, None] * received.astype(jnp.float32)
    mixed = (
        jnp.zeros((tok_rows, width), jnp.float32).at[slot_token].add(weighted).astype(jnp.bfloat16)
    )

    def restore(recv):
        return (
            jnp.zeros((hidden_rows, width), jnp.bfloat16)
            .at[send_order]
            .set(recv.reshape(hidden_rows, width))
        )

    return (mixed, restore(back_g), restore(back_u), restore(back_v))


def solution(mesh):
    return jax.shard_map(
        local,
        mesh=mesh,
        in_specs=(
            P("expert", "dp"),
            P("expert", "dp"),
            P("expert", None),
            P("expert", None),
            P("expert", "dp"),
            P("expert", "dp"),
            P("expert", "dp"),
            P(),
        ),
        out_specs=(P("expert", "dp"), P("expert", "dp"), P("expert", "dp"), P("expert", "dp")),
        check_vma=False,
    )
```

profile of v0, /device:TPU:1, one launch (start us, length us, event | category | flops | bytes accessed | tf_op | source)
XLA Modules:
  0.0 443.0 jit_solution(12090451229990088704)
XLA Ops:
  8.0 3.8 sort.35
  11.8 2.6 gather_fusion.4
  14.4 18.8 %all-to-all-start.3 = ((bf16[48,8,512]{2,1,0:T(8,128)(2,1)}), bf16[48,8,512]{2,1,0:T(8,128)(2,1)S(1)}, u32[]{:S(2)}, u32[]{:S(2)}) async-start(bf16[48,8,512]{2,1,0:T(8,128)(2,1)} %bitcast.8), calls=%async_computation.3 | async-start | bytes 786432 | tf_op jit(solution)/shard_map/all_to_all | solution.py:30
  33.3 2.6 gather_fusion.2
  35.9 17.4 %all-to-all-done.3 = bf16[48,8,512]{2,1,0:T(8,128)(2,1)S(1)} async-done(((bf16[48,8,512]{2,1,0:T(8,128)(2,1)}), bf16[48,8,512]{2,1,0:T(8,128)(2,1)S(1)}, u32[]{:S(2)}, u32[]{:S(2)}) %all-to-all-start.3) | async-done | bytes 393248 | tf_op jit(solution)/shard_map/all_to_all | solution.py:30
  53.3 6.0 %all-to-all-start.1 = ((bf16[48,8,512]{2,1,0:T(8,128)(2,1)}), bf16[48,8,512]{2,1,0:T(8,128)(2,1)S(1)}, u32[]{:S(2)}, u32[]{:S(2)}) async-start(bf16[48,8,512]{2,1,0:T(8,128)(2,1)} %bitcast.4), calls=%async_computation.1 | async-start | bytes 786432 | tf_op jit(solution)/shard_map/all_to_all | solution.py:30
  61.1 2.6 gather_fusion.3
  63.7 14.9 %all-to-all-done.1 = bf16[48,8,512]{2,1,0:T(8,128)(2,1)S(1)} async-done(((bf16[48,8,512]{2,1,0:T(8,128)(2,1)}), bf16[48,8,512]{2,1,0:T(8,128)(2,1)S(1)}, u32[]{:S(2)}, u32[]{:S(2)}) %all-to-all-start.1) | async-done | bytes 393248 | tf_op jit(solution)/shard_map/all_to_all | solution.py:30
  78.7 6.6 %all-to-all-start.2 = ((bf16[48,8,512]{2,1,0:T(8,128)(2,1)}), bf16[48,8,512]{2,1,0:T(8,128)(2,1)S(1)}, u32[]{:S(2)}, u32[]{:S(2)}) async-start(bf16[48,8,512]{2,1,0:T(8,128)(2,1)} %bitcast.6), calls=%async_computation.2 | async-start | bytes 786432 | tf_op jit(solution)/shard_map/all_to_all | solution.py:30
  85.4 1.4 scatter_custom_fusion
  86.9 3.5 gather_fusion
  90.5 2.1 gather_fusion.1
  92.9 1.1 broadcast_select_fusion
  93.9 10.4 %all-to-all-done.2 = bf16[48,8,512]{2,1,0:T(8,128)(2,1)S(1)} async-done(((bf16[48,8,512]{2,1,0:T(8,128)(2,1)}), bf16[48,8,512]{2,1,0:T(8,128)(2,1)S(1)}, u32[]{:S(2)}, u32[]{:S(2)}) %all-to-all-start.2) | async-done | bytes 393248 | tf_op jit(solution)/shard_map/all_to_all | solution.py:30
  104.4 6.6 %all-to-all-start = ((bf16[48,10,512]{2,1,0:T(8,128)(2,1)}), bf16[48,10,512]{2,1,0:T(8,128)(2,1)S(1)}, u32[]{:S(2)}, u32[]{:S(2)}) async-start(bf16[48,10,512]{2,1,0:T(8,128)(2,1)} %broadcast_select_fusion), calls=%async_computation | async-start | bytes 1572864 | tf_op jit(solution)/shard_map/all_to_all | solution.py:57
  111.1 2.6 gather_fusion.5
  113.7 1.2 reshape.205
  114.9 1.0 multiply_convert_fusion
  116.0 26.6 %all-to-all-done = bf16[48,10,512]{2,1,0:T(8,128)(2,1)S(1)} async-done(((bf16[48,10,512]{2,1,0:T(8,128)(2,1)}), bf16[48,10,512]{2,1,0:T(8,128)(2,1)S(1)}, u32[]{:S(2)}, u32[]{:S(2)}) %all-to-all-start) | async-done | bytes 491552 | tf_op jit(solution)/shard_map/all_to_all | solution.py:57
  142.5 6.5 %all-to-all-start.5 = ((bf16[48,10,512]{2,1,0:T(8,128)(2,1)}), bf16[48,10,512]{2,1,0:T(8,128)(2,1)S(1)}, u32[]{:S(2)}, u32[]{:S(2)}) async-start(bf16[48,10,512]{2,1,0:T(8,128)(2,1)} %multiply_convert_fusion), calls=%async_computation.5 | async-start | bytes 1572864 | tf_op jit(solution)/shard_map/all_to_all | solution.py:64
  150.7 5.7 %sort.37.cloned.1.call-done = (s32[48,384]{1,0:T(8,128)}, s32[48,384]{1,0:T(8,128)}) async-done(((s32[48,384]{1,0:T(8,128)}, s32[48,384]{1,0:T(8,128)}), (s32[48,384]{1,0:T(8,128)}, s32[48,384]{1,0:T(8,128)})) %sort.37.cloned.1.call-update) | async-done | bytes 147472 | tf_op jit(solution)/shard_map/jit(argsort)/sort | solution.py:35
  157.3 3.4 gather_fusion.9
  161.8 2.0 scatter_custom_fusion.3
  163.8 2.0 scatter_custom_fusion.1
  165.9 2.7 scatter_custom_fusion.2
  168.8 1.3 fusion.36
  170.1 1.3 fusion.37
  171.4 9.3 %all-to-all-done.5 = bf16[48,10,512]{2,1,0:T(8,128)(2,1)S(1)} async-done(((bf16[48,10,512]{2,1,0:T(8,128)(2,1)}), bf16[48,10,512]{2,1,0:T(8,128)(2,1)S(1)}, u32[]{:S(2)}, u32[]{:S(2)}) %all-to-all-start.5) | async-done | bytes 491552 | tf_op jit(solution)/shard_map/all_to_all | solution.py:64
  180.9 1.3 fusion.38
  182.2 123.1 %all-reduce.3.cloned.1.call-done = (f32[480,384]{1,0:T(8,128)}, f32[480,384]{1,0:T(8,128)}, f32[480,384]{1,0:T(8,128)}) async-done(((f32[480,384]{1,0:T(8,128)}, f32[480,384]{1,0:T(8,128)}, f32[480,384]{1,0:T(8,128)}), (f32[480,384]{1,0:T(8,128)}, f32[480,384]{1,0:T(8,128)}, f32[480,384]{1,0:T(8,128)})) %all-reduce.3.cloned.1.call-update) | async-done | bytes 2211856 | tf_op jit(solution)/shard_map/psum | solution.py:78
  305.3 1.5 multiply_convert_fusion.3
  307.3 2.6 gather_fusion.8
  309.8 13.0 %all-to-all-start.8 = ((bf16[48,8,512]{2,1,0:T(8,128)(2,1)}), bf16[48,8,512]{2,1,0:T(8,128)(2,1)S(1)}, u32[]{:S(2)}, u32[]{:S(2)}) async-start(bf16[48,8,512]{2,1,0:T(8,128)(2,1)} %bitcast.14), calls=%async_computation.8 | async-start | bytes 786432 | tf_op jit(solution)/shard_map/all_to_all | solution.py:102
  322.8 1.8 convolution_convert_fusion.2
  324.6 2.6 gather_fusion.7
  327.2 15.7 %all-to-all-done.8 = bf16[48,8,512]{2,1,0:T(8,128)(2,1)S(1)} async-done(((bf16[48,8,512]{2,1,0:T(8,128)(2,1)}), bf16[48,8,512]{2,1,0:T(8,128)(2,1)S(1)}, u32[]{:S(2)}, u32[]{:S(2)}) %all-to-all-start.8) | async-done | bytes 393248 | tf_op jit(solution)/shard_map/all_to_all | solution.py:102
  342.9 6.0 %all-to-all-start.7 = ((bf16[48,8,512]{2,1,0:T(8,128)(2,1)}), bf16[48,8,512]{2,1,0:T(8,128)(2,1)S(1)}, u32[]{:S(2)}, u32[]{:S(2)}) async-start(bf16[48,8,512]{2,1,0:T(8,128)(2,1)} %bitcast.12), calls=%async_computation.7 | async-start | bytes 786432 | tf_op jit(solution)/shard_map/all_to_all | solution.py:102
  348.9 2.1 convolution_convert_fusion.3
  351.0 2.6 gather_fusion.6
  353.6 14.6 %all-to-all-done.7 = bf16[48,8,512]{2,1,0:T(8,128)(2,1)S(1)} async-done(((bf16[48,8,512]{2,1,0:T(8,128)(2,1)}), bf16[48,8,512]{2,1,0:T(8,128)(2,1)S(1)}, u32[]{:S(2)}, u32[]{:S(2)}) %all-to-all-start.7) | async-done | bytes 393248 | tf_op jit(solution)/shard_map/all_to_all | solution.py:102
  368.1 6.5 %all-to-all-start.6 = ((bf16[48,8,512]{2,1,0:T(8,128)(2,1)}), bf16[48,8,512]{2,1,0:T(8,128)(2,1)S(1)}, u32[]{:S(2)}, u32[]{:S(2)}) async-start(bf16[48,8,512]{2,1,0:T(8,128)(2,1)} %bitcast.10), calls=%async_computation.6 | async-start | bytes 786432 | tf_op jit(solution)/shard_map/all_to_all | solution.py:102
  376.1 17.5 %all-to-all-done.6 = bf16[48,8,512]{2,1,0:T(8,128)(2,1)S(1)} async-done(((bf16[48,8,512]{2,1,0:T(8,128)(2,1)}), bf16[48,8,512]{2,1,0:T(8,128)(2,1)S(1)}, u32[]{:S(2)}, u32[]{:S(2)}) %all-to-all-start.6) | async-done | bytes 393248 | tf_op jit(solution)/shard_map/all_to_all | solution.py:102
  393.6 6.4 %all-to-all-start.4 = ((bf16[48,10,512]{2,1,0:T(8,128)(2,1)}), bf16[48,10,512]{2,1,0:T(8,128)(2,1)S(1)}, u32[]{:S(2)}, u32[]{:S(2)}) async-start(bf16[48,10,512]{2,1,0:T(8,128)(2,1)} %reshape.196), calls=%async_computation.4 | async-start | bytes 1572864 | tf_op jit(solution)/shard_map/all_to_all | solution.py:102
  400.1 2.7 scatter_custom_fusion.7
  402.7 2.7 scatter_custom_fusion.6
  405.4 2.7 scatter_custom_fusion.5
  408.1 23.6 %all-to-all-done.4 = bf16[48,10,512]{2,1,0:T(8,128)(2,1)S(1)} async-done(((bf16[48,10,512]{2,1,0:T(8,128)(2,1)}), bf16[48,10,512]{2,1,0:T(8,128)(2,1)S(1)}, u32[]{:S(2)}, u32[]{:S(2)}) %all-to-all-start.4) | async-done | bytes 491552 | tf_op jit(solution)/shard_map/all_to_all | solution.py:102
  431.9 3.6 scatter_custom_fusion.4
  (73 shorter events, 9.7 us)
Async XLA Ops:
  7.2 4.7 %copy-start = (bf16[384,512]{1,0:T(8,128)(2,1)S(1)}, bf16[384,512]{1,0:T(8,128)(2,1)}, u32[]{:S(2)}) copy-start(bf16[384,512]{1,0:T(8,128)(2,1)} %param.14) | copy-start | bytes 1179652
  11.8 21.4 %copy-start.3 = (bf16[384,512]{1,0:T(8,128)(2,1)S(1)}, bf16[384,512]{1,0:T(8,128)(2,1)}, u32[]{:S(2)}) copy-start(bf16[384,512]{1,0:T(8,128)(2,1)} %param.12) | copy-start | bytes 1179652
  14.4 38.9 %all-to-all-start.3 = ((bf16[48,8,512]{2,1,0:T(8,128)(2,1)}), bf16[48,8,512]{2,1,0:T(8,128)(2,1)S(1)}, u32[]{:S(2)}, u32[]{:S(2)}) async-start(bf16[48,8,512]{2,1,0:T(8,128)(2,1)} %bitcast.8), calls=%async_computation.3 | async-start | bytes 786432 | tf_op jit(solution)/shard_map/all_to_all | solution.py:30
  33.3 26.1 %copy-start.11 = (s32[128,2]{0,1:T(2,128)S(1)}, s32[128,2]{0,1:T(2,128)}, u32[]{:S(2)}) copy-start(s32[128,2]{0,1:T(2,128)} %param.10) | copy-start | bytes 3076
  33.3 27.6 %copy-start.12 = (f32[128,2]{0,1:T(2,128)S(1)}, f32[128,2]{0,1:T(2,128)}, u32[]{:S(2)}) copy-start(f32[128,2]{0,1:T(2,128)} %param.11) | copy-start | bytes 3076
  35.9 25.3 %copy-start.4 = (bf16[384,512]{1,0:T(8,128)(2,1)S(1)}, bf16[384,512]{1,0:T(8,128)(2,1)}, u32[]{:S(2)}) copy-start(bf16[384,512]{1,0:T(8,128)(2,1)} %param.13) | copy-start | bytes 1179652
  53.3 25.4 %all-to-all-start.1 = ((bf16[48,8,512]{2,1,0:T(8,128)(2,1)}), bf16[48,8,512]{2,1,0:T(8,128)(2,1)S(1)}, u32[]{:S(2)}, u32[]{:S(2)}) async-start(bf16[48,8,512]{2,1,0:T(8,128)(2,1)} %bitcast.4), calls=%async_computation.1 | async-start | bytes 786432 | tf_op jit(solution)/shard_map/all_to_all | solution.py:30
  63.7 26.8 %copy-start.1 = (bf16[128,512]{1,0:T(8,128)(2,1)S(1)}, bf16[128,512]{1,0:T(8,128)(2,1)}, u32[]{:S(2)}) copy-start(bf16[128,512]{1,0:T(8,128)(2,1)} %param.8) | copy-start | bytes 393220
  78.7 11.9 %copy-start.5 = (bf16[48,8,512]{2,1,0:T(8,128)(2,1)}, bf16[48,8,512]{2,1,0:T(8,128)(2,1)S(1)}, u32[]{:S(2)}) copy-start(bf16[48,8,512]{2,1,0:T(8,128)(2,1)S(1)} %all-to-all-done.1) | copy-start | bytes 1179652
  78.7 25.7 %all-to-all-start.2 = ((bf16[48,8,512]{2,1,0:T(8,128)(2,1)}), bf16[48,8,512]{2,1,0:T(8,128)(2,1)S(1)}, u32[]{:S(2)}, u32[]{:S(2)}) async-start(bf16[48,8,512]{2,1,0:T(8,128)(2,1)} %bitcast.6), calls=%async_computation.2 | async-start | bytes 786432 | tf_op jit(solution)/shard_map/all_to_all | solution.py:30
  92.8 18.3 %copy-start.2 = (bf16[128,512]{1,0:T(8,128)(2,1)S(1)}, bf16[128,512]{1,0:T(8,128)(2,1)}, u32[]{:S(2)}) copy-start(bf16[128,512]{1,0:T(8,128)(2,1)} %param.9) | copy-start | bytes 393220
  104.4 6.8 %copy-start.7 = (bf16[48,8,512]{2,1,0:T(8,128)(2,1)}, bf16[48,8,512]{2,1,0:T(8,128)(2,1)S(1)}, u32[]{:S(2)}) copy-start(bf16[48,8,512]{2,1,0:T(8,128)(2,1)S(1)} %all-to-all-done.2) | copy-start | bytes 1179652
  104.4 38.2 %all-to-all-start = ((bf16[48,10,512]{2,1,0:T(8,128)(2,1)}), bf16[48,10,512]{2,1,0:T(8,128)(2,1)S(1)}, u32[]{:S(2)}, u32[]{:S(2)}) async-start(bf16[48,10,512]{2,1,0:T(8,128)(2,1)} %broadcast_select_fusion), calls=%async_computation | async-start | bytes 1572864 | tf_op jit(solution)/shard_map/all_to_all | solution.py:57
  114.9 34.2 %copy-start.10 = (s32[18432]{0:T(1024)S(1)}, s32[18432]{0:T(1024)}, u32[]{:S(2)}) copy-start(s32[18432]{0:T(1024)} %param.15) | copy-start | bytes 221188
  142.5 38.2 %all-to-all-start.5 = ((bf16[48,10,512]{2,1,0:T(8,128)(2,1)}), bf16[48,10,512]{2,1,0:T(8,128)(2,1)S(1)}, u32[]{:S(2)}, u32[]{:S(2)}) async-start(bf16[48,10,512]{2,1,0:T(8,128)(2,1)} %multiply_convert_fusion), calls=%async_computation.5 | async-start | bytes 1572864 | tf_op jit(solution)/shard_map/all_to_all | solution.py:64
  149.1 7.4 %sort.37.cloned.1.call-start = ((), (), s32[]{:S(2)}) async-start(), calls=%async_computation.10 | async-start | bytes 442400 | tf_op jit(solution)/shard_map/jit(argsort)/sort | solution.py:35
  150.5 154.8 %all-reduce.3.cloned.1.call-start = ((), (), s32[]{:S(2)}) async-start(), calls=%async_computation.9 | async-start | bytes 4423680 | tf_op jit(solution)/shard_map/psum | solution.py:78
  157.3 6.5 %copy-start.6 = (bf16[48,8,512]{2,1,0:T(8,128)(2,1)S(1)}, bf16[48,8,512]{2,1,0:T(8,128)(2,1)}, u32[]{:S(2)}) copy-start(bf16[48,8,512]{2,1,0:T(8,128)(2,1)} %copy-done.5) | copy-start | bytes 1179652
  160.8 5.1 %copy-start.8 = (bf16[48,8,512]{2,1,0:T(8,128)(2,1)S(1)}, bf16[48,8,512]{2,1,0:T(8,128)(2,1)}, u32[]{:S(2)}) copy-start(bf16[48,8,512]{2,1,0:T(8,128)(2,1)} %copy-done.7) | copy-start | bytes 1179652
  168.7 1.3 copy-start.9
  309.8 33.0 %all-to-all-start.8 = ((bf16[48,8,512]{2,1,0:T(8,128)(2,1)}), bf16[48,8,512]{2,1,0:T(8,128)(2,1)S(1)}, u32[]{:S(2)}, u32[]{:S(2)}) async-start(bf16[48,8,512]{2,1,0:T(8,128)(2,1)} %bitcast.14), calls=%async_computation.8 | async-start | bytes 786432 | tf_op jit(solution)/shard_map/all_to_all | solution.py:102
  342.9 25.3 %all-to-all-start.7 = ((bf16[48,8,512]{2,1,0:T(8,128)(2,1)}), bf16[48,8,512]{2,1,0:T(8,128)(2,1)S(1)}, u32[]{:S(2)}, u32[]{:S(2)}) async-start(bf16[48,8,512]{2,1,0:T(8,128)(2,1)} %bitcast.12), calls=%async_computation.7 | async-start | bytes 786432 | tf_op jit(solution)/shard_map/all_to_all | solution.py:102
  368.1 25.5 %all-to-all-start.6 = ((bf16[48,8,512]{2,1,0:T(8,128)(2,1)}), bf16[48,8,512]{2,1,0:T(8,128)(2,1)S(1)}, u32[]{:S(2)}, u32[]{:S(2)}) async-start(bf16[48,8,512]{2,1,0:T(8,128)(2,1)} %bitcast.10), calls=%async_computation.6 | async-start | bytes 786432 | tf_op jit(solution)/shard_map/all_to_all | solution.py:102
  393.6 38.1 %all-to-all-start.4 = ((bf16[48,10,512]{2,1,0:T(8,128)(2,1)}), bf16[48,10,512]{2,1,0:T(8,128)(2,1)S(1)}, u32[]{:S(2)}, u32[]{:S(2)}) async-start(bf16[48,10,512]{2,1,0:T(8,128)(2,1)} %reshape.196), calls=%async_computation.4 | async-start | bytes 1572864 | tf_op jit(solution)/shard_map/all_to_all | solution.py:102
Sparse Core Ops, SparseCore 0:
  152.9 3.3 sort.39.cloned.1.call-done
  182.4 122.9 all-reduce.2
  (1 shorter events, 0.0 us)
where the time goes:
time: 449 us; the launch traced here: 443 us
  waiting for transfers between devices  273 us (61%)
  starting transfers between devices  76.8 us (17%)
  local copies, waits for them, and re-layouts  54.3 us (12%)
  other arithmetic  15.6 us (3%)
  between operations  14.5 us (3%)
  matrix products  8.62 us (2%)
    psum x1, waiting for transfers between devices, local(): gate, upval, backward_pass = lax.psum((part_g, part_u, part_q), 'dp')  123 us
    all_to_all x4, waiting for transfers between devices, local(): lax.all_to_all(for_sending(sent), 'expert', split_axis=0, concat_axis=0,...  71.4 us
    all_to_all x3, waiting for transfers between devices, local(): lax.all_to_all(for_sending(outgoing), 'expert', split_axis=0, concat_axis...  42.7 us
    all_to_all x4, starting transfers between devices, local(): lax.all_to_all(for_sending(sent), 'expert', split_axis=0, concat_axis=0,...  31.9 us
    all_to_all x3, starting transfers between devices, local(): lax.all_to_all(for_sending(outgoing), 'expert', split_axis=0, concat_axis...  31.5 us
    all_to_all x1, waiting for transfers between devices, local(): lax.all_to_all(send_x.reshape(owners, capacity, width), 'expert', split_a...  26.6 us
    all_to_all x1, waiting for transfers between devices, local(): lax.all_to_all(send_c.reshape(owners, capacity, width), 'expert', split_a...  9.32 us
  transfers between devices with their start and end apart: 10, of which 10 were waited for; matrix products, arithmetic and copies ran while one was open for 12% of the time, Pallas kernels for 0%

commit v1 on v0

v1 whole, which is shorter than its diff:
```python
import functools

import jax
import jax.numpy as jnp
from jax import lax
from jax.experimental import pallas as pl
from jax.experimental.pallas import tpu as pltpu
from jax.sharding import PartitionSpec as P

BF = jnp.bfloat16
F32 = jnp.float32
NX = 4
LANE = 128
META = 16
BLK = 2 * LANE + META
GROUP = 8


def layer_kernel(
    Z,
    Y,
    meta_ref,
    tok_ref,
    cot_ref,
    wg_ref,
    wu_ref,
    wv_ref,
    ecol_ref,
    erow_ref,
    mixed_ref,
    gg_ref,
    gu_ref,
    gv_ref,
    TS,
    XB,
    WS,
    WB,
    VT,
    GS,
    PB,
    RB,
    HB,
    DD,
    ACC,
    OUT,
    MF,
    MB,
    MR,
    SS,
    SB,
    SL,
    SE,
    FS,
    FB,
    GO,
    GR,
    PT,
    x_send,
    x_recv,
    z_send,
    z_recv,
    s_send,
    s_recv,
    w_send,
    w_recv,
    p_send,
    p_recv,
    h_send,
    h_recv,
    m_send,
    m_recv,
    r_send,
    r_recv,
    f_send,
    f_recv,
    g_send,
    g_recv,
):
    E = Z * NX
    R = GROUP * E
    NH = Z // 2
    PAIRS = E // 2
    HALF = 2 * LANE
    dp = lax.axis_index("dp")
    ex = lax.axis_index("expert")
    y, c = dp // 2, dp % 2
    z, x = ex // NX, ex % NX
    other = 1 - c
    side = x // 2

    def dev(zz, xx, yy, cc):
        return (yy * 2 + cc, zz * NX + xx)

    z_next = dev((z + 1) % Z, x, y, c)
    z_prev = dev((z + Z - 1) % Z, x, y, c)
    sibling = dev(z, x, y, other)

    def remote(src, dst, send, recv, target):
        return pltpu.make_async_remote_copy(
            src_ref=src,
            dst_ref=dst,
            send_sem=send,
            recv_sem=recv,
            device_id=target,
            device_id_type=pl.DeviceIdType.MESH,
        )

    def wait_for(ref, sem):
        pltpu.make_async_copy(ref, ref, sem).wait()

    barrier = pltpu.get_barrier_semaphore()
    greeted = [z_next, z_prev]
    for dx in range(NX):
        for dc in range(2):
            if dx or dc:
                greeted.append(dev(z, (x + dx) % NX, y, (c + dc) % 2))
        for dy in range(1, Y):
            greeted.append(dev(z, (x + dx) % NX, (y + dy) % Y, c))
    for g in greeted:
        pl.semaphore_signal(barrier, inc=1, device_id=g, device_id_type=pl.DeviceIdType.MESH)

    for b in range(NX):
        lanes = slice(b * LANE, (b + 1) * LANE)
        TS[b, 0:LANE, :] = tok_ref[:, lanes]
        TS[b, LANE : LANE + META, :] = meta_ref[...]
        TS[b, LANE + META : BLK, :] = cot_ref[:, lanes]
    XB[0, x, c] = TS[x]
    pl.semaphore_wait(barrier, len(greeted))

    for dx in range(1, NX):
        to = (x + dx) % NX
        remote(
            TS.at[to], XB.at[0, x, c], x_send, x_recv.at[dx - 1], dev(z, to, y, c)
        ).start()

    ecol, erow = ecol_ref[...], erow_ref[...]
    same = ecol == erow
    i0 = lax.broadcasted_iota(jnp.int32, (R, R), 0)
    i1 = lax.broadcasted_iota(jnp.int32, (R, R), 1)
    rank_row = jnp.sum(jnp.where(same & (i0 < i1), 1.0, 0.0), axis=0, keepdims=True)
    rank_col = jnp.sum(jnp.where(same & (i1 < i0), 1.0, 0.0), axis=1, keepdims=True)
    pos_row = erow * GROUP + rank_row.astype(jnp.int32)
    pos_col = ecol * GROUP + rank_col.astype(jnp.int32)
    perm = jnp.where(i0 == pos_row, 1.0, 0.0).astype(BF)
    PT[...] = jnp.where(i1 == pos_col, 1.0, 0.0).astype(BF)
    for a, w_ref in enumerate((wg_ref, wu_ref, wv_ref)):
        for b in range(NX):
            lanes = slice(b * LANE, (b + 1) * LANE)
            WS[a, b] = jnp.dot(perm, w_ref[:, lanes], preferred_element_type=F32).astype(BF)
        for dx in range(NX):
            to = (x + dx) % NX
            copy = remote(
                WS.at[a, to],
                WB.at[a, x % 2, c],
                w_send.at[a, dx],
                w_recv.at[a, x % 2, c],
                dev(z, to, y, side),
            )
            if dx:
                copy.start()
            else:

                @pl.when(c == side)
                def _():
                    WB[a, x % 2, c] = WS[a, x]

                @pl.when(c != side)
                def _():
                    copy.start()

    ACC[...] = jnp.zeros_like(ACC)
    for way in range(2):
        for half in range(2):
            first = NH if way == half else NH - 1
            SB[way, half, first] = jnp.zeros((LANE, HALF), BF)

    def forward(s, tau):
        remote(
            XB.at[s, tau, c],
            XB.at[s + 1, tau, c],
            z_send.at[s],
            z_recv.at[s + 1, tau],
            z_next if tau < 2 else z_prev,
        ).start()

    def share(s, tau):
        remote(XB.at[s, tau, c], XB.at[s, tau, c], s_send.at[s], s_recv.at[s], sibling).start()

    for dx in range(1, NX):
        wait_for(XB.at[0, (x + NX - dx) % NX, c], x_recv.at[dx - 1])
    for tau in (0, 2, 1, 3):
        forward(0, tau)
    for tau in range(NX):
        share(0, tau)

    for a in range(3):
        for i in range(2):
            for cc in range(2):

                @pl.when(jnp.logical_not((2 * c + i == x) & (cc == c)))
                def _():
                    wait_for(WB.at[a, i, cc], w_recv.at[a, i, cc])

    for i in range(2):
        for cc in range(2):
            VT[cc * LANE : (cc + 1) * LANE, i * R : (i + 1) * R] = jnp.transpose(
                WB[2, i, cc].astype(F32)
            ).astype(BF)

    def arrive(s):
        for tau in (0, 2, 1, 3):
            wait_for(XB.at[s, tau, c], z_recv.at[s, tau])

            @pl.when(s < Z - 1)
            def _():
                forward(s, tau)

            share(s, tau)

    sub = lax.broadcasted_iota(jnp.int32, (16, LANE), 0) // 8

    def named(s, tau):
        rows = XB[s, tau, c, LANE : LANE + META, :].astype(F32)
        return [
            (jnp.broadcast_to(rows[k : k + 1, :], (16, LANE)) - sub.astype(F32)).astype(BF)
            for k in range(2)
        ]

    def owner_of(s, tau):
        return tau, (tau + s) % Y

    def project(s):
        wait_for(XB.at[s, :, other], s_recv.at[s])
        for h in range(2):
            taus = (2 * h, 2 * h + 1)

            def rows_of(first):
                return jnp.concatenate(
                    [
                        jnp.concatenate(
                            [XB[s, tau, cc, first : first + LANE, :] for cc in range(2)], axis=1
                        )
                        for tau in taus
                    ],
                    axis=0,
                )

            for first, arrays in ((0, (0, 1)), (LANE + META, (2,))):
                right = rows_of(first)
                for a in arrays:
                    for i in range(2):
                        left = jnp.concatenate([WB[a, i, 0], WB[a, i, 1]], axis=1)
                        GS[a * 2 + i] = lax.dot_general(
                            left,
                            right,
                            (((1,), (1,)), ((), ())),
                            preferred_element_type=F32,
                        ).astype(BF)
            for p, tau in enumerate(taus):
                lanes = slice(p * LANE, (p + 1) * LANE)
                who = named(s, tau)
                kept = [[jnp.zeros((16, LANE), BF) for _ in range(6)] for _ in range(2)]
                for m in range(PAIRS):
                    hits = [who[k] == jnp.asarray(2 * m, BF) for k in range(2)]
                    for q in range(6):
                        value = GS[q, 16 * m : 16 * m + 16, lanes]
                        for k in range(2):
                            kept[k][q] = jnp.where(hits[k], value, kept[k][q])
                for a in range(3):
                    for k in range(2):
                        parts = []
                        for i in range(2):
                            v = kept[k][a * 2 + i].astype(F32)
                            parts.append(v[0:8] + v[8:16])
                        PB[s, tau, a * 32 + k * 16 : a * 32 + k * 16 + 16, :] = jnp.concatenate(
                            parts, axis=0
                        ).astype(BF)
        for tau in range(NX):
            ox, oy = owner_of(s, tau)
            slot = ((x - ox + NX) % NX) * Y + (y - oy + Y) % Y

            @pl.when(slot != 0)
            def _():
                remote(
                    PB.at[s, tau],
                    RB.at[s // Y, slot - 1],
                    p_send.at[s],
                    p_recv.at[s // Y],
                    dev(z, ox, oy, c),
                ).start()

    def activate(s):
        wait_for(RB.at[s // Y], p_recv.at[s // Y])
        total = PB[s, x].astype(F32)
        for slot in range(NX * Y - 1):
            total = total + RB[s // Y, slot].astype(F32)
        meta = XB[s, x, c, LANE : LANE + META, :].astype(F32)
        for k in range(2):
            w = meta[2 + 3 * k : 3 + 3 * k] + meta[3 + 3 * k : 4 + 3 * k] + meta[4 + 3 * k : 5 + 3 * k]
            gate = total[k * 16 : k * 16 + 16]
            up = total[32 + k * 16 : 48 + k * 16]
            back = total[64 + k * 16 : 80 + k * 16] * w
            sig = 1.0 / (1.0 + jnp.exp(-gate))
            HB[s, x, k * 16 : k * 16 + 16, :] = (
                back * up * sig * (1.0 + gate * (1.0 - sig))
            ).astype(BF)
            HB[s, x, 32 + k * 16 : 48 + k * 16, :] = (back * gate * sig).astype(BF)
            HB[s, x, 64 + k * 16 : 80 + k * 16, :] = (w * (gate * sig * up)).astype(BF)
        for dx in range(NX):
            for dy in range(Y):
                if dx or dy:
                    remote(
                        HB.at[s, x],
                        HB.at[s, x],
                        h_send.at[s // Y],
                        h_recv.at[s, x],
                        dev(z, (x + dx) % NX, (y + dy) % Y, c),
                    ).start()

    def apply(s):
        for tau in range(NX):
            ox, oy = owner_of(s, tau)

            @pl.when(jnp.logical_not((ox == x) & (oy == y)))
            def _():
                wait_for(HB.at[s, tau], h_recv.at[s, tau])

        for tau in range(NX):
            lanes = slice(tau * LANE, (tau + 1) * LANE)
            who = named(s, tau)
            twice = []
            for a in range(3):
                for k in range(2):
                    v = HB[s, tau, a * 32 + k * 16 : a * 32 + k * 16 + 16, :].astype(F32)
                    for i in range(2):
                        v8 = v[8 * i : 8 * i + 8]
                        twice.append(jnp.concatenate([v8, v8], axis=0).astype(BF))
            zero = jnp.zeros((16, LANE), BF)
            for m in range(PAIRS):
                hits = [who[k] == jnp.asarray(2 * m, BF) for k in range(2)]
                for a in range(3):
                    for i in range(2):
                        DD[a, i * R + 16 * m : i * R + 16 * m + 16, lanes] = jnp.where(
                            hits[0],
                            twice[a * 4 + i],
                            jnp.where(hits[1], twice[a * 4 + 2 + i], zero),
                        )
        out = jnp.dot(VT[...], DD[2], preferred_element_type=F32)
        OUT[0] = out[0:LANE]
        OUT[1] = out[LANE : 2 * LANE]
        MB[s] = OUT[other].astype(BF)
        remote(MB.at[s], MR.at[s], m_send.at[s], m_recv.at[s], sibling).start()
        MF[s] = OUT[c]
        for first, arrays in ((0, (0, 1)), (LANE + META, (2,))):
            right = jnp.concatenate(
                [
                    jnp.concatenate(
                        [XB[s, tau, cc, first : first + LANE, :] for cc in range(2)], axis=1
                    )
                    for tau in range(NX)
                ],
                axis=0,
            )
            for a in arrays:
                ACC[a] += jnp.dot(DD[a], right, preferred_element_type=F32)

    def own_output(s, half):
        lanes = slice(half * HALF, (half + 1) * HALF)
        return MF[s, :, lanes] + MR[s, :, lanes].astype(F32)

    def pass_on(d):
        def flow(way, half):
            first = NH if way == half else NH - 1

            @pl.when(d < first)
            def _():
                wait_for(SB.at[way, half, d], r_recv.at[way, half, d])

            s = d if way == half else Z - d
            total = own_output(s, half) + SB[way, half, d].astype(F32)

            @pl.when(d == 1)
            def _():
                SL[way, half] = total
                remote(
                    SL.at[way, half],
                    SE.at[way, half],
                    r_send.at[way, half, 1],
                    r_recv.at[way, half, 0],
                    z_prev if way == 0 else z_next,
                ).start()

            @pl.when(d > 1)
            def _():
                SS[way, half, d] = total.astype(BF)
                remote(
                    SS.at[way, half, d],
                    SB.at[way, half, d - 1],
                    r_send.at[way, half, d],
                    r_recv.at[way, half, d - 1],
                    z_prev if way == 0 else z_next,
                ).start()

        flow(0, 0)
        flow(1, 1)

        @pl.when(d < NH)
        def _():
            flow(0, 1)
            flow(1, 0)

    def step(it, carry):
        @pl.when((it >= 1) & (it < Z))
        def _():
            arrive(it)

        @pl.when((it >= 2) & (it < Z + 2))
        def _():
            s = it - 2

            @pl.when((x + s) % Y == y)
            def _():
                activate(s)

        @pl.when((it >= 1) & (it < Z + 1))
        def _():
            project(it - 1)

        @pl.when((it >= 4 + NH) & (it < Z + 4))
        def _():
            s = it - 4
            wait_for(MR.at[s], m_recv.at[s])
            @pl.when(s > NH)
            def _():
                wait_for(MR.at[Z - s], m_recv.at[Z - s])
            pass_on(Z - s)

        @pl.when((it >= 3) & (it < Z + 3))
        def _():
            apply(it - 3)

        return carry

    lax.fori_loop(1, Z + 4, step, 0)

    for a in range(3):
        for i in range(2):
            for cc in range(2):
                GO[a, i, cc] = ACC[a, i * R : (i + 1) * R, cc * LANE : (cc + 1) * LANE].astype(BF)
        for i in range(2):
            for cc in range(2):
                mine = (2 * c + i == x) & (cc == c)

                @pl.when(jnp.logical_not(mine))
                def _():
                    remote(
                        GO.at[a, i, cc],
                        GR.at[a, x],
                        g_send.at[a, i, cc],
                        g_recv.at[a, x],
                        dev(z, 2 * c + i, y, cc),
                    ).start()

                @pl.when(mine)
                def _():
                    GR[a, x] = GO[a, i, cc]

    wait_for(MR.at[0], m_recv.at[0])
    for way in range(2):
        for half in range(2):
            wait_for(SE.at[way, half], r_recv.at[way, half, 0])
    for half in range(2):
        done = (
            own_output(0, half) + SE[0, half] + SE[1, half]
        ).astype(BF)
        for p in range(2):
            FS[2 * half + p] = done[:, p * LANE : (p + 1) * LANE]
    for dx in range(1, NX):
        to = (x + dx) % NX
        remote(FS.at[to], FB.at[x], f_send.at[dx - 1], f_recv.at[dx - 1], dev(z, to, y, c)).start()
    FB[x] = FS[x]
    for dx in range(1, NX):
        wait_for(FB.at[(x + NX - dx) % NX], f_recv.at[dx - 1])
    for b in range(NX):
        mixed_ref[:, b * LANE : (b + 1) * LANE] = jnp.transpose(FB[b].astype(F32)).astype(BF)

    for a, out_ref in enumerate((gg_ref, gu_ref, gv_ref)):
        for dx in range(NX):
            frm = (x + dx) % NX
            if dx:
                wait_for(GR.at[a, frm], g_recv.at[a, frm])
            else:

                @pl.when(c != side)
                def _():
                    wait_for(GR.at[a, frm], g_recv.at[a, frm])

        for b in range(NX):
            out_ref[:, b * LANE : (b + 1) * LANE] = jnp.dot(
                PT[...], GR[a, b], preferred_element_type=F32
            ).astype(BF)

    wait_for(TS.at[0 : NX - 1], x_send)
    for s in range(Z):
        if s < Z - 1:
            wait_for(XB.at[s, :, c], z_send.at[s])
        wait_for(XB.at[s, :, c], s_send.at[s])
        wait_for(MR.at[s], m_send.at[s])
        owned = (x + s) % Y == y

        @pl.when(owned)
        def _():
            wait_for(PB.at[s, 0 : NX - 1], p_send.at[s])
            wait_for(RB.at[s // Y], h_send.at[s // Y])

        @pl.when(jnp.logical_not(owned))
        def _():
            wait_for(PB.at[s], p_send.at[s])

    for a in range(3):
        for dx in range(NX):
            if dx:
                wait_for(WS.at[a, 0], w_send.at[a, dx])
            else:

                @pl.when(c != side)
                def _():
                    wait_for(WS.at[a, 0], w_send.at[a, 0])

        for i in range(2):
            for cc in range(2):

                @pl.when(jnp.logical_not((2 * c + i == x) & (cc == c)))
                def _():
                    wait_for(GO.at[a, i, cc], g_send.at[a, i, cc])

    for dx in range(1, NX):
        wait_for(FS.at[0], f_send.at[dx - 1])
    for way in range(2):
        for half in range(2):
            first = NH if way == half else NH - 1
            wait_for(SL.at[way, half], r_send.at[way, half, 1])
            for d in range(2, first + 1):
                wait_for(SS.at[way, half, d], r_send.at[way, half, d])


def local(Z, Y, tokens, cotangent, routes, route_weight, gate_dense, up_dense, down_dense, slice_map):
    rows, width = gate_dense.shape
    E = Z * NX
    here = lax.axis_index("expert")
    own = lax.dynamic_slice_in_dim(slice_map, here * rows, rows) // rows
    high = lax.reduce_precision(route_weight, 8, 7)
    rest = route_weight - high
    mid = lax.reduce_precision(rest, 8, 7)
    low = rest - mid
    pieces = [routes.astype(F32)] + [
        jnp.stack([high[:, k], mid[:, k], low[:, k]], axis=1) for k in range(2)
    ]
    meta = jnp.concatenate(pieces + [jnp.zeros((LANE, META - 8), F32)], axis=1).T.astype(BF)
    dma = pltpu.SemaphoreType.DMA
    NH = Z // 2
    scratch = [
        pltpu.VMEM((NX, BLK, LANE), BF),
        pltpu.VMEM((Z, NX, 2, BLK, LANE), BF),
        pltpu.VMEM((3, NX, rows, LANE), BF),
        pltpu.VMEM((3, 2, 2, rows, LANE), BF),
        pltpu.VMEM((2 * LANE, 2 * rows), BF),
        pltpu.VMEM((6, rows, 2 * LANE), BF),
        pltpu.VMEM((Z, NX, 96, LANE), BF),
        pltpu.VMEM((-(-Z // Y), NX * Y - 1, 96, LANE), BF),
        pltpu.VMEM((Z, NX, 96, LANE), BF),
        pltpu.VMEM((3, 2 * rows, 4 * LANE), BF),
        pltpu.VMEM((3, 2 * rows, 2 * LANE), F32),
        pltpu.VMEM((2, LANE, 4 * LANE), F32),
        pltpu.VMEM((Z, LANE, 4 * LANE), F32),
        pltpu.VMEM((Z, LANE, 4 * LANE), BF),
        pltpu.VMEM((Z, LANE, 4 * LANE), BF),
        pltpu.VMEM((2, 2, NH + 1, LANE, 2 * LANE), BF),
        pltpu.VMEM((2, 2, NH + 1, LANE, 2 * LANE), BF),
        pltpu.VMEM((2, 2, LANE, 2 * LANE), F32),
        pltpu.VMEM((2, 2, LANE, 2 * LANE), F32),
        pltpu.VMEM((NX, LANE, LANE), BF),
        pltpu.VMEM((NX, LANE, LANE), BF),
        pltpu.VMEM((3, 2, 2, rows, LANE), BF),
        pltpu.VMEM((3, NX, rows, LANE), BF),
        pltpu.VMEM((rows, rows), BF),
        dma,
        dma((NX - 1,)),
        dma((Z,)),
        dma((Z, NX)),
        dma((Z,)),
        dma((Z,)),
        dma((3, NX)),
        dma((3, 2, 2)),
        dma((Z,)),
        dma((-(-Z // Y),)),
        dma((-(-Z // Y),)),
        dma((Z, NX)),
        dma((Z,)),
        dma((Z,)),
        dma((2, 2, NH + 1)),
        dma((2, 2, NH + 1)),
        dma((NX - 1,)),
        dma((NX - 1,)),
        dma((3, 2, 2)),
        dma((3, NX)),
    ]
    vmem = pl.BlockSpec(memory_space=pltpu.VMEM)
    return pl.pallas_call(
        functools.partial(layer_kernel, Z, Y),
        out_shape=(
            jax.ShapeDtypeStruct(tokens.shape, BF),
            jax.ShapeDtypeStruct(gate_dense.shape, BF),
            jax.ShapeDtypeStruct(gate_dense.shape, BF),
            jax.ShapeDtypeStruct(gate_dense.shape, BF),
        ),
        in_specs=[vmem] * 8,
        out_specs=(vmem,) * 4,
        scratch_shapes=scratch,
        compiler_params=pltpu.CompilerParams(
            collective_id=0, has_side_effects=True, vmem_limit_bytes=52 * 1024 * 1024
        ),
    )(
        meta,
        tokens,
        cotangent,
        gate_dense,
        up_dense,
        down_dense,
        own.reshape(rows, 1),
        own.reshape(1, rows),
    )


def solution(mesh):
    Y = mesh.shape["dp"] // 2
    Z = mesh.shape["expert"] // NX
    return jax.shard_map(
        functools.partial(local, Z, Y),
        mesh=mesh,
        in_specs=(
            P("expert", "dp"),
            P("expert", "dp"),
            P("expert", None),
            P("expert", None),
            P("expert", "dp"),
            P("expert", "dp"),
            P("expert", "dp"),
            P(),
        ),
        out_specs=(P("expert", "dp"), P("expert", "dp"), P("expert", "dp"), P("expert", "dp")),
        check_vma=False,
    )
```

time: 449 us -> 237 us (0.53); the launches traced: 443 us -> 236 us
  waiting for transfers between devices: 273 us -> 0 us
  Pallas kernels: 0 us -> 230 us
  starting transfers between devices: 76.8 us -> 0 us
  local copies, waits for them, and re-layouts: 54.3 us -> 3.08 us
  between operations: 14.5 us -> 0.71 us
  other arithmetic: 15.6 us -> 2.2 us
  matrix products: 8.62 us -> 0 us
    pallas_call x0 -> x1, Pallas kernels: none -> 230 us  [local(): pl.pallas_call(functools.partial(layer_kernel, Z, Y), out_shape=(jax.Shap...]
    all_to_all x9 -> x0, waiting for transfers between devices: 150 us -> none  [the longest x4 71.4 us: local(): lax.all_to_all(for_sending(sent), 'expert', split_axis=0, concat_axis=0,...]
    psum x1 -> x0, waiting for transfers between devices: 123 us -> none  [local(): gate, upval, backward_pass = lax.psum((part_g, part_u, part_q), 'dp')]
    all_to_all x9 -> x0, starting transfers between devices: 76.6 us -> none  [the longest x4 31.9 us: local(): lax.all_to_all(for_sending(sent), 'expert', split_axis=0, concat_axis=0,...]
    gather x13 -> x0, local copies, waits for them, and re-layouts: 27.5 us -> none  [the longest x3 7.75 us: local(): w[send_order].reshape(owners, group, width)]
    scatter x7 -> x0, local copies, waits for them, and re-layouts: 16.1 us -> none  [the longest x3 8 us: restore(): return jnp.zeros((hidden_rows, width), jnp.bfloat16).at[send_order].set(r...]
    dot_general x7 -> x0, matrix products: 8.62 us -> none  [the longest x1 2.11 us: local(): lax.dot_general(dgate, inputs, rowsum, preferred_element_type=jnp.float32)]
    sort x2 -> x0, local copies, waits for them, and re-layouts: 5.76 us -> none  [local(): jnp.argsort(jnp.where(mine, 0, 1).astype(jnp.int32), axis=1, stable=True)]
  transfers between devices with their start and end apart: 10 -> 0, of which waited for: 10 -> 0; matrix products, arithmetic and copies ran while one was open for 12% -> 0% of each run, Pallas kernels for 0% -> 0%
where the time goes in v1:
time: 237 us; the launch traced here: 236 us
  Pallas kernels  230 us (97%)
  local copies, waits for them, and re-layouts  3.08 us (1%)
    pallas_call x1, Pallas kernels, local(): pl.pallas_call(functools.partial(layer_kernel, Z, Y), out_shape=(jax.Shap...  230 us

profile of v1, /device:TPU:1, one launch (start us, length us, event | category | flops | bytes accessed | tf_op | source)
XLA Modules:
  0.0 236.3 jit_solution(3646363841534950053)
XLA Ops:
  0.6 0.0 copy-start.1
  0.6 0.0 copy-start
  0.7 0.7 convert_convert_fusion
  1.4 0.8 add_select_fusion
  2.2 0.7 fusion.1
  2.9 0.1 reshape.16.ecol_ref
  3.1 0.0 copy-done.1
  3.1 0.0 copy-done
  3.1 230.3 %shard_map.111 = (bf16[128,512]{1,0:T(8,128)(2,1)S(1)}, bf16[384,512]{1,0:T(8,128)(2,1)S(1)}, bf16[384,512]{1,0:T(8,128)(2,1)S(1)}, bf16[384,512]{1,0:T(8,128)(2,1)S(1)}) custom-call(bf16[16,128]{1,0:T(8,128)(2,1)S(1)} %bitcast.1, bf16[128,512]{1,0:T(8,128)(2,1)S(1)} %copy-done, bf16[128,512]{1,0:T(8,128)(2,1)S(1)} %copy-done.1, bf16[384,512]{1,0:T(8,128)(2,1)} %wg_ref.1, ...), custom_call_target="tpu_custom_call" | custom-call | tf_op jit(solution)/shard_map/pallas_call | solution.py:609
  233.4 0.7 copy.17
  234.0 0.7 copy.18
  234.8 0.7 copy.19
  235.5 0.7 copy.20
  (5 shorter events, 0.1 us)
Async XLA Ops:
  0.6 2.4 %copy-start.1 = (bf16[128,512]{1,0:T(8,128)(2,1)S(1)}, bf16[128,512]{1,0:T(8,128)(2,1)}, u32[]{:S(2)}) copy-start(bf16[128,512]{1,0:T(8,128)(2,1)} %cot_ref.1) | copy-start | bytes 393220
  0.6 2.4 %copy-start = (bf16[128,512]{1,0:T(8,128)(2,1)S(1)}, bf16[128,512]{1,0:T(8,128)(2,1)}, u32[]{:S(2)}) copy-start(bf16[128,512]{1,0:T(8,128)(2,1)} %tok_ref.1) | copy-start | bytes 393220

commit v2 on v1

--- a/solution.py
+++ b/solution.py
@@ -38,7 +38,9 @@
     VT,
     GS,
     PB,
-    RB,
+    RX,
+    YS,
+    YR,
     HB,
     DD,
     ACC,
@@ -65,6 +67,8 @@
     w_recv,
     p_send,
     p_recv,
+    y_send,
+    y_recv,
     h_send,
     h_recv,
     m_send,
@@ -114,8 +118,8 @@
         for dc in range(2):
             if dx or dc:
                 greeted.append(dev(z, (x + dx) % NX, y, (c + dc) % 2))
-        for dy in range(1, Y):
-            greeted.append(dev(z, (x + dx) % NX, (y + dy) % Y, c))
+    for dy in range(1, Y):
+        greeted.append(dev(z, x, (y + dy) % Y, c))
     for g in greeted:
         pl.semaphore_signal(barrier, inc=1, device_id=g, device_id_type=pl.DeviceIdType.MESH)
 
@@ -221,13 +225,7 @@
 
     def named(s, tau):
         rows = XB[s, tau, c, LANE : LANE + META, :].astype(F32)
-        return [
-            (jnp.broadcast_to(rows[k : k + 1, :], (16, LANE)) - sub.astype(F32)).astype(BF)
-            for k in range(2)
-        ]
-
-    def owner_of(s, tau):
-        return tau, (tau + s) % Y
+        return [jnp.broadcast_to(rows[k : k + 1, :], (16, LANE)) for k in range(2)]
 
     def project(s):
         wait_for(XB.at[s, :, other], s_recv.at[s])
@@ -255,45 +253,41 @@
                             right,
                             (((1,), (1,)), ((), ())),
                             preferred_element_type=F32,
-                        ).astype(BF)
+                        )
             for p, tau in enumerate(taus):
                 lanes = slice(p * LANE, (p + 1) * LANE)
-                who = named(s, tau)
-                kept = [[jnp.zeros((16, LANE), BF) for _ in range(6)] for _ in range(2)]
-                for m in range(PAIRS):
-                    hits = [who[k] == jnp.asarray(2 * m, BF) for k in range(2)]
+                who = [w[0:8] for w in named(s, tau)]
+                kept = [[jnp.zeros((8, LANE), F32) for _ in range(6)] for _ in range(2)]
+                for e in range(E):
+                    hits = [who[k] == float(e) for k in range(2)]
                     for q in range(6):
-                        value = GS[q, 16 * m : 16 * m + 16, lanes]
+                        value = GS[q, 8 * e : 8 * e + 8, lanes]
                         for k in range(2):
                             kept[k][q] = jnp.where(hits[k], value, kept[k][q])
                 for a in range(3):
                     for k in range(2):
-                        parts = []
                         for i in range(2):
-                            v = kept[k][a * 2 + i].astype(F32)
-                            parts.append(v[0:8] + v[8:16])
-                        PB[s, tau, a * 32 + k * 16 : a * 32 + k * 16 + 16, :] = jnp.concatenate(
-                            parts, axis=0
-                        ).astype(BF)
-        for tau in range(NX):
-            ox, oy = owner_of(s, tau)
-            slot = ((x - ox + NX) % NX) * Y + (y - oy + Y) % Y
-
-            @pl.when(slot != 0)
-            def _():
-                remote(
-                    PB.at[s, tau],
-                    RB.at[s // Y, slot - 1],
-                    p_send.at[s],
-                    p_recv.at[s // Y],
-                    dev(z, ox, oy, c),
-                ).start()
+                            row = a * 32 + k * 16 + i * 8
+                            PB[s, tau, row : row + 8, :] = kept[k][a * 2 + i]
+        for dx in range(1, NX):
+            to = (x + dx) % NX
+            remote(
+                PB.at[s, to], RX.at[s, dx - 1], p_send.at[s], p_recv.at[s], dev(z, to, y, c)
+            ).start()
+
+    def sum_x(s):
+        wait_for(RX.at[s], p_recv.at[s])
+        YS[s] = (PB[s, x] + RX[s, 0] + RX[s, 1] + RX[s, 2]).astype(BF)
+        for dy in range(1, Y):
+            remote(
+                YS.at[s], YR.at[s, dy - 1], y_send.at[s], y_recv.at[s], dev(z, x, (y + dy) % Y, c)
+            ).start()
 
     def activate(s):
-        wait_for(RB.at[s // Y], p_recv.at[s // Y])
-        total = PB[s, x].astype(F32)
-        for slot in range(NX * Y - 1):
-            total = total + RB[s // Y, slot].astype(F32)
+        wait_for(YR.at[s], y_recv.at[s])
+        total = YS[s].astype(F32)
+        for slot in range(Y - 1):
+            total = total + YR[s, slot].astype(F32)
         meta = XB[s, x, c, LANE : LANE + META, :].astype(F32)
         for k in range(2):
             w = meta[2 + 3 * k : 3 + 3 * k] + meta[3 + 3 * k : 4 + 3 * k] + meta[4 + 3 * k : 5 + 3 * k]
@@ -306,28 +300,21 @@
             ).astype(BF)
             HB[s, x, 32 + k * 16 : 48 + k * 16, :] = (back * gate * sig).astype(BF)
             HB[s, x, 64 + k * 16 : 80 + k * 16, :] = (w * (gate * sig * up)).astype(BF)
-        for dx in range(NX):
-            for dy in range(Y):
-                if dx or dy:
-                    remote(
-                        HB.at[s, x],
-                        HB.at[s, x],
-                        h_send.at[s // Y],
-                        h_recv.at[s, x],
-                        dev(z, (x + dx) % NX, (y + dy) % Y, c),
-                    ).start()
+        for dx in range(1, NX):
+            remote(
+                HB.at[s, x], HB.at[s, x], h_send.at[s], h_recv.at[s, x], dev(z, (x + dx) % NX, y, c)
+            ).start()
 
     def apply(s):
         for tau in range(NX):
-            ox, oy = owner_of(s, tau)
-
-            @pl.when(jnp.logical_not((ox == x) & (oy == y)))
+
+            @pl.when(tau != x)
             def _():
                 wait_for(HB.at[s, tau], h_recv.at[s, tau])
 
         for tau in range(NX):
             lanes = slice(tau * LANE, (tau + 1) * LANE)
-            who = named(s, tau)
+            who = [(w - sub.astype(F32)).astype(BF) for w in named(s, tau)]
             twice = []
             for a in range(3):
                 for k in range(2):
@@ -414,34 +401,36 @@
         def _():
             arrive(it)
 
-        @pl.when((it >= 2) & (it < Z + 2))
-        def _():
-            s = it - 2
-
-            @pl.when((x + s) % Y == y)
-            def _():
-                activate(s)
-
         @pl.when((it >= 1) & (it < Z + 1))
         def _():
             project(it - 1)
 
-        @pl.when((it >= 4 + NH) & (it < Z + 4))
+        @pl.when((it >= 2) & (it < Z + 2))
         def _():
-            s = it - 4
+            sum_x(it - 2)
+
+        @pl.when((it >= 3) & (it < Z + 3))
+        def _():
+            activate(it - 3)
+
+        @pl.when((it >= 5 + NH) & (it < Z + 5))
+        def _():
+            s = it - 5
             wait_for(MR.at[s], m_recv.at[s])
+
             @pl.when(s > NH)
             def _():
                 wait_for(MR.at[Z - s], m_recv.at[Z - s])
+
             pass_on(Z - s)
 
-        @pl.when((it >= 3) & (it < Z + 3))
+        @pl.when((it >= 4) & (it < Z + 4))
         def _():
-            apply(it - 3)
+            apply(it - 4)
 
         return carry
 
-    lax.fori_loop(1, Z + 4, step, 0)
+    lax.fori_loop(1, Z + 5, step, 0)
 
     for a in range(3):
         for i in range(2):
@@ -506,17 +495,9 @@
             wait_for(XB.at[s, :, c], z_send.at[s])
         wait_for(XB.at[s, :, c], s_send.at[s])
         wait_for(MR.at[s], m_send.at[s])
-        owned = (x + s) % Y == y
-
-        @pl.when(owned)
-        def _():
-            wait_for(PB.at[s, 0 : NX - 1], p_send.at[s])
-            wait_for(RB.at[s // Y], h_send.at[s // Y])
-
-        @pl.when(jnp.logical_not(owned))
-        def _():
-            wait_for(PB.at[s], p_send.at[s])
-
+        wait_for(RX.at[s], p_send.at[s])
+        wait_for(YR.at[s], y_send.at[s])
+        wait_for(HB.at[s, 0 : NX - 1], h_send.at[s])
     for a in range(3):
         for dx in range(NX):
             if dx:
@@ -565,9 +546,11 @@
         pltpu.VMEM((3, NX, rows, LANE), BF),
         pltpu.VMEM((3, 2, 2, rows, LANE), BF),
         pltpu.VMEM((2 * LANE, 2 * rows), BF),
-        pltpu.VMEM((6, rows, 2 * LANE), BF),
-        pltpu.VMEM((Z, NX, 96, LANE), BF),
-        pltpu.VMEM((-(-Z // Y), NX * Y - 1, 96, LANE), BF),
+        pltpu.VMEM((6, rows, 2 * LANE), F32),
+        pltpu.VMEM((Z, NX, 96, LANE), F32),
+        pltpu.VMEM((Z, NX - 1, 96, LANE), F32),
+        pltpu.VMEM((Z, 96, LANE), BF),
+        pltpu.VMEM((Z, Y - 1, 96, LANE), BF),
         pltpu.VMEM((Z, NX, 96, LANE), BF),
         pltpu.VMEM((3, 2 * rows, 4 * LANE), BF),
         pltpu.VMEM((3, 2 * rows, 2 * LANE), F32),
@@ -593,8 +576,10 @@
         dma((3, NX)),
         dma((3, 2, 2)),
         dma((Z,)),
-        dma((-(-Z // Y),)),
-        dma((-(-Z // Y),)),
+        dma((Z,)),
+        dma((Z,)),
+        dma((Z,)),
+        dma((Z,)),
         dma((Z, NX)),
         dma((Z,)),
         dma((Z,)),

time: 237 us -> 146 us (0.62)
  Pallas kernels: 230 us -> 140 us
    pallas_call x1, Pallas kernels: 230 us -> 140 us  [local(): pl.pallas_call(functools.partial(layer_kernel, Z, Y), out_shape=(jax.Shap...]
where the time goes in v2:
time: 146 us; the launch traced here: 145 us
  Pallas kernels  140 us (96%)
  local copies, waits for them, and re-layouts  3.08 us (2%)
  other arithmetic  2.2 us (2%)
    pallas_call x1, Pallas kernels, local(): pl.pallas_call(functools.partial(layer_kernel, Z, Y), out_shape=(jax.Shap...  140 us

profile of v2, /device:TPU:1, one launch (start us, length us, event | category | flops | bytes accessed | tf_op | source)
XLA Modules:
  0.0 145.5 jit_solution(14033575630540758120)
XLA Ops:
  0.6 0.0 copy-start.1
  0.6 0.0 copy-start
  0.7 0.7 convert_convert_fusion
  1.4 0.8 add_select_fusion
  2.2 0.7 fusion.1
  2.9 0.1 reshape.16.ecol_ref
  3.1 0.0 copy-done.1
  3.1 0.0 copy-done
  3.1 139.5 %shard_map.111 = (bf16[128,512]{1,0:T(8,128)(2,1)S(1)}, bf16[384,512]{1,0:T(8,128)(2,1)S(1)}, bf16[384,512]{1,0:T(8,128)(2,1)S(1)}, bf16[384,512]{1,0:T(8,128)(2,1)S(1)}) custom-call(bf16[16,128]{1,0:T(8,128)(2,1)S(1)} %bitcast.1, bf16[128,512]{1,0:T(8,128)(2,1)S(1)} %copy-done, bf16[128,512]{1,0:T(8,128)(2,1)S(1)} %copy-done.1, bf16[384,512]{1,0:T(8,128)(2,1)} %wg_ref.1, ...), custom_call_target="tpu_custom_call" | custom-call | tf_op jit(solution)/shard_map/pallas_call | solution.py:594
  142.6 0.7 copy.17
  143.3 0.7 copy.18
  144.0 0.7 copy.19
  144.7 0.7 copy.20
  (5 shorter events, 0.1 us)
Async XLA Ops:
  0.6 2.4 %copy-start.1 = (bf16[128,512]{1,0:T(8,128)(2,1)S(1)}, bf16[128,512]{1,0:T(8,128)(2,1)}, u32[]{:S(2)}) copy-start(bf16[128,512]{1,0:T(8,128)(2,1)} %cot_ref.1) | copy-start | bytes 393220
  0.6 2.4 %copy-start = (bf16[128,512]{1,0:T(8,128)(2,1)S(1)}, bf16[128,512]{1,0:T(8,128)(2,1)}, u32[]{:S(2)}) copy-start(bf16[128,512]{1,0:T(8,128)(2,1)} %tok_ref.1) | copy-start | bytes 393220

commit v3 on v2

--- a/solution.py
+++ b/solution.py
@@ -39,6 +39,8 @@
     GS,
     PB,
     RX,
+    YP,
+    YQ,
     YS,
     YR,
     HB,
@@ -67,6 +69,8 @@
     w_recv,
     p_send,
     p_recv,
+    q_send,
+    q_recv,
     y_send,
     y_recv,
     h_send,
@@ -147,6 +151,35 @@
     pos_col = ecol * GROUP + rank_col.astype(jnp.int32)
     perm = jnp.where(i0 == pos_row, 1.0, 0.0).astype(BF)
     PT[...] = jnp.where(i1 == pos_col, 1.0, 0.0).astype(BF)
+    def forward(s, tau):
+        remote(
+            XB.at[s, tau, c],
+            XB.at[s + 1, tau, c],
+            z_send.at[s],
+            z_recv.at[s + 1, tau],
+            z_next if tau < 2 else z_prev,
+        ).start()
+
+    def share(s, tau):
+        remote(XB.at[s, tau, c], XB.at[s, tau, c], s_send.at[s], s_recv.at[s], sibling).start()
+
+    for dx in range(1, NX):
+        wait_for(XB.at[0, (x + NX - dx) % NX, c], x_recv.at[dx - 1])
+    for tau in (0, 2, 1, 3):
+        forward(0, tau)
+    for tau in range(NX):
+        share(0, tau)
+
+    def arrive(s):
+        for tau in (0, 2, 1, 3):
+            wait_for(XB.at[s, tau, c], z_recv.at[s, tau])
+
+            @pl.when(s < Z - 1)
+            def _():
+                forward(s, tau)
+
+            share(s, tau)
+
     for a, w_ref in enumerate((wg_ref, wu_ref, wv_ref)):
         for b in range(NX):
             lanes = slice(b * LANE, (b + 1) * LANE)
@@ -178,24 +211,7 @@
             first = NH if way == half else NH - 1
             SB[way, half, first] = jnp.zeros((LANE, HALF), BF)
 
-    def forward(s, tau):
-        remote(
-            XB.at[s, tau, c],
-            XB.at[s + 1, tau, c],
-            z_send.at[s],
-            z_recv.at[s + 1, tau],
-            z_next if tau < 2 else z_prev,
-        ).start()
-
-    def share(s, tau):
-        remote(XB.at[s, tau, c], XB.at[s, tau, c], s_send.at[s], s_recv.at[s], sibling).start()
-
-    for dx in range(1, NX):
-        wait_for(XB.at[0, (x + NX - dx) % NX, c], x_recv.at[dx - 1])
-    for tau in (0, 2, 1, 3):
-        forward(0, tau)
-    for tau in range(NX):
-        share(0, tau)
+    arrive(1)
 
     for a in range(3):
         for i in range(2):
@@ -210,16 +226,6 @@
             VT[cc * LANE : (cc + 1) * LANE, i * R : (i + 1) * R] = jnp.transpose(
                 WB[2, i, cc].astype(F32)
             ).astype(BF)
-
-    def arrive(s):
-        for tau in (0, 2, 1, 3):
-            wait_for(XB.at[s, tau, c], z_recv.at[s, tau])
-
-            @pl.when(s < Z - 1)
-            def _():
-                forward(s, tau)
-
-            share(s, tau)
 
     sub = lax.broadcasted_iota(jnp.int32, (16, LANE), 0) // 8
 
@@ -277,16 +283,27 @@
 
     def sum_x(s):
         wait_for(RX.at[s], p_recv.at[s])
-        YS[s] = (PB[s, x] + RX[s, 0] + RX[s, 1] + RX[s, 2]).astype(BF)
-        for dy in range(1, Y):
+        YP[s] = PB[s, x] + RX[s, 0] + RX[s, 1] + RX[s, 2]
+        remote(
+            YP.at[s], YQ.at[s], q_send.at[s], q_recv.at[s], dev(z, x, y + 1 - 2 * (y % 2), c)
+        ).start()
+
+    def sum_pair(s):
+        wait_for(YQ.at[s], q_recv.at[s])
+        YS[s] = (YP[s] + YQ[s]).astype(BF)
+        for pair in range(1, Y // 2):
             remote(
-                YS.at[s], YR.at[s, dy - 1], y_send.at[s], y_recv.at[s], dev(z, x, (y + dy) % Y, c)
+                YS.at[s],
+                YR.at[s, pair - 1],
+                y_send.at[s],
+                y_recv.at[s],
+                dev(z, x, (y + 2 * pair) % Y, c),
             ).start()
 
     def activate(s):
         wait_for(YR.at[s], y_recv.at[s])
-        total = YS[s].astype(F32)
-        for slot in range(Y - 1):
+        total = YP[s] + YQ[s]
+        for slot in range(Y // 2 - 1):
             total = total + YR[s, slot].astype(F32)
         meta = XB[s, x, c, LANE : LANE + META, :].astype(F32)
         for k in range(2):
@@ -397,9 +414,9 @@
             flow(1, 0)
 
     def step(it, carry):
-        @pl.when((it >= 1) & (it < Z))
-        def _():
-            arrive(it)
+        @pl.when(it < Z - 1)
+        def _():
+            arrive(it + 1)
 
         @pl.when((it >= 1) & (it < Z + 1))
         def _():
@@ -411,11 +428,15 @@
 
         @pl.when((it >= 3) & (it < Z + 3))
         def _():
-            activate(it - 3)
-
-        @pl.when((it >= 5 + NH) & (it < Z + 5))
-        def _():
-            s = it - 5
+            sum_pair(it - 3)
+
+        @pl.when((it >= 4) & (it < Z + 4))
+        def _():
+            activate(it - 4)
+
+        @pl.when(it >= 6 + NH)
+        def _():
+            s = it - 6
             wait_for(MR.at[s], m_recv.at[s])
 
             @pl.when(s > NH)
@@ -424,9 +445,9 @@
 
             pass_on(Z - s)
 
-        @pl.when((it >= 4) & (it < Z + 4))
-        def _():
-            apply(it - 4)
+        @pl.when(it >= 5)
+        def _():
+            apply(it - 5)
 
         return carry
 
@@ -453,6 +474,10 @@
                 @pl.when(mine)
                 def _():
                     GR[a, x] = GO[a, i, cc]
+
+    wait_for(MR.at[Z - 1], m_recv.at[Z - 1])
+    wait_for(MR.at[1], m_recv.at[1])
+    pass_on(1)
 
     wait_for(MR.at[0], m_recv.at[0])
     for way in range(2):
@@ -497,6 +522,7 @@
         wait_for(MR.at[s], m_send.at[s])
         wait_for(RX.at[s], p_send.at[s])
         wait_for(YR.at[s], y_send.at[s])
+        wait_for(YQ.at[s], q_send.at[s])
         wait_for(HB.at[s, 0 : NX - 1], h_send.at[s])
     for a in range(3):
         for dx in range(NX):
@@ -549,8 +575,10 @@
         pltpu.VMEM((6, rows, 2 * LANE), F32),
         pltpu.VMEM((Z, NX, 96, LANE), F32),
         pltpu.VMEM((Z, NX - 1, 96, LANE), F32),
+        pltpu.VMEM((Z, 96, LANE), F32),
+        pltpu.VMEM((Z, 96, LANE), F32),
         pltpu.VMEM((Z, 96, LANE), BF),
-        pltpu.VMEM((Z, Y - 1, 96, LANE), BF),
+        pltpu.VMEM((Z, Y // 2 - 1, 96, LANE), BF),
         pltpu.VMEM((Z, NX, 96, LANE), BF),
         pltpu.VMEM((3, 2 * rows, 4 * LANE), BF),
         pltpu.VMEM((3, 2 * rows, 2 * LANE), F32),
@@ -575,6 +603,8 @@
         dma((Z,)),
         dma((3, NX)),
         dma((3, 2, 2)),
+        dma((Z,)),
+        dma((Z,)),
         dma((Z,)),
         dma((Z,)),
         dma((Z,)),

time: 146 us -> 143 us (0.979)
  Pallas kernels: 140 us -> 136 us
    pallas_call x1, Pallas kernels: 140 us -> 136 us  [local(): pl.pallas_call(functools.partial(layer_kernel, Z, Y), out_shape=(jax.Shap...]
where the time goes in v3:
time: 143 us; the launch traced here: 142 us
  Pallas kernels  136 us (95%)
  local copies, waits for them, and re-layouts  3.08 us (2%)
  other arithmetic  2.2 us (2%)
    pallas_call x1, Pallas kernels, local(): pl.pallas_call(functools.partial(layer_kernel, Z, Y), out_shape=(jax.Shap...  136 us
    unnamed x8, local copies, waits for them, and re-layouts  2.9 us

profile of v3, /device:TPU:1, one launch (start us, length us, event | category | flops | bytes accessed | tf_op | source)
XLA Modules:
  0.0 142.4 jit_solution(7504661393569767854)
XLA Ops:
  0.6 0.0 copy-start.1
  0.6 0.0 copy-start
  0.7 0.7 convert_convert_fusion
  1.4 0.8 add_select_fusion
  2.2 0.7 fusion.1
  2.9 0.1 reshape.16.ecol_ref
  3.1 0.0 copy-done.1
  3.1 0.0 copy-done
  3.1 136.4 %shard_map.111 = (bf16[128,512]{1,0:T(8,128)(2,1)S(1)}, bf16[384,512]{1,0:T(8,128)(2,1)S(1)}, bf16[384,512]{1,0:T(8,128)(2,1)S(1)}, bf16[384,512]{1,0:T(8,128)(2,1)S(1)}) custom-call(bf16[16,128]{1,0:T(8,128)(2,1)S(1)} %bitcast.1, bf16[128,512]{1,0:T(8,128)(2,1)S(1)} %copy-done, bf16[128,512]{1,0:T(8,128)(2,1)S(1)} %copy-done.1, bf16[384,512]{1,0:T(8,128)(2,1)} %wg_ref.1, ...), custom_call_target="tpu_custom_call" | custom-call | tf_op jit(solution)/shard_map/pallas_call | solution.py:624
  139.5 0.7 copy.17
  140.2 0.7 copy.18
  140.9 0.7 copy.19
  141.6 0.7 copy.20
  (5 shorter events, 0.1 us)
Async XLA Ops:
  0.6 2.4 %copy-start.1 = (bf16[128,512]{1,0:T(8,128)(2,1)S(1)}, bf16[128,512]{1,0:T(8,128)(2,1)}, u32[]{:S(2)}) copy-start(bf16[128,512]{1,0:T(8,128)(2,1)} %cot_ref.1) | copy-start | bytes 393220
  0.6 2.4 %copy-start = (bf16[128,512]{1,0:T(8,128)(2,1)S(1)}, bf16[128,512]{1,0:T(8,128)(2,1)}, u32[]{:S(2)}) copy-start(bf16[128,512]{1,0:T(8,128)(2,1)} %tok_ref.1) | copy-start | bytes 393220

commit v4 on v3

--- a/solution.py
+++ b/solution.py
@@ -211,7 +211,8 @@
             first = NH if way == half else NH - 1
             SB[way, half, first] = jnp.zeros((LANE, HALF), BF)
 
-    arrive(1)
+    for s in range(1, 4):
+        arrive(s)
 
     for a in range(3):
         for i in range(2):
@@ -414,9 +415,9 @@
             flow(1, 0)
 
     def step(it, carry):
-        @pl.when(it < Z - 1)
-        def _():
-            arrive(it + 1)
+        @pl.when(it < Z - 3)
+        def _():
+            arrive(it + 3)
 
         @pl.when((it >= 1) & (it < Z + 1))
         def _():

time: 143 us -> 142 us (level)
  no operation moved by 1% of the time
where the time goes in v4:
time: 142 us
  Pallas kernels  136 us (96%)
  local copies, waits for them, and re-layouts  3.08 us (2%)
  other arithmetic  2.2 us (2%)
    pallas_call x1, Pallas kernels, local(): pl.pallas_call(functools.partial(layer_kernel, Z, Y), out_shape=(jax.Shap...  136 us
    unnamed x8, local copies, waits for them, and re-layouts  2.9 us

profile of v4, /device:TPU:1, one launch (start us, length us, event | category | flops | bytes accessed | tf_op | source)
XLA Modules:
  0.0 142.2 jit_solution(8688147756860149293)
XLA Ops:
  0.6 0.0 copy-start.1
  0.6 0.0 copy-start
  0.7 0.7 convert_convert_fusion
  1.4 0.8 add_select_fusion
  2.2 0.7 fusion.1
  2.9 0.1 reshape.16.ecol_ref
  3.1 0.0 copy-done.1
  3.1 0.0 copy-done
  3.1 136.2 %shard_map.111 = (bf16[128,512]{1,0:T(8,128)(2,1)S(1)}, bf16[384,512]{1,0:T(8,128)(2,1)S(1)}, bf16[384,512]{1,0:T(8,128)(2,1)S(1)}, bf16[384,512]{1,0:T(8,128)(2,1)S(1)}) custom-call(bf16[16,128]{1,0:T(8,128)(2,1)S(1)} %bitcast.1, bf16[128,512]{1,0:T(8,128)(2,1)S(1)} %copy-done, bf16[128,512]{1,0:T(8,128)(2,1)S(1)} %copy-done.1, bf16[384,512]{1,0:T(8,128)(2,1)} %wg_ref.1, ...), custom_call_target="tpu_custom_call" | custom-call | tf_op jit(solution)/shard_map/pallas_call | solution.py:625
  139.3 0.7 copy.17
  140.0 0.7 copy.18
  140.7 0.7 copy.19
  141.4 0.7 copy.20
  (5 shorter events, 0.1 us)
Async XLA Ops:
  0.6 2.4 %copy-start.1 = (bf16[128,512]{1,0:T(8,128)(2,1)S(1)}, bf16[128,512]{1,0:T(8,128)(2,1)}, u32[]{:S(2)}) copy-start(bf16[128,512]{1,0:T(8,128)(2,1)} %cot_ref.1) | copy-start | bytes 393220
  0.6 2.4 %copy-start = (bf16[128,512]{1,0:T(8,128)(2,1)S(1)}, bf16[128,512]{1,0:T(8,128)(2,1)}, u32[]{:S(2)}) copy-start(bf16[128,512]{1,0:T(8,128)(2,1)} %tok_ref.1) | copy-start | bytes 393220
